TPU v7x, 32 devices: a whole 2x2x4 slice. The times are simulated.
32 devices in a mesh: row: 4 (over y, x), col: 8 (over z, core).
Axes of the slice: x: 2, y: 2, z: 4, core: 2. Of those that a mesh axis runs over, the one named last changes fastest.
Arguments:
- eigvecs: float32 [512, 65536], P('col', 'row'), may hold values from -6 to 6
- reflectors: float32 [3, 256, 65536], P(None, 'col', 'row'), may hold values from -0.0234375 to 0.0234375
- factors: float32 [3, 256, 256], P(None, 'col'), may hold values from -1 to 2, as said below
Outputs:
- transformed: float32 [512, 65536], P('col', 'row')
Inputs may be any that keep to these rules, and one draw needn't show every extreme that they name: factors[b] is upper triangular with diagonal entries between 1 and 2.
All inputs are finite; a program needn't handle non-finite values.
Results may differ from a plain program's by a relative error of at most 0.00012.
Values sent between devices are 32-bit elements; how exact they have to be, the bound alone decides.
A program may use at most 128 MiB of HBM per device.

v0:
```python
import jax
import jax.numpy as jnp
from jax import lax
from jax.sharding import PartitionSpec as P


def matmul(left, right):
    return jnp.dot(left, right, precision=lax.Precision.HIGHEST, preferred_element_type=jnp.float32)


def inner_last(left, right):
    return lax.dot_general(
        left,
        right,
        (((1,), (1,)), ((), ())),
        precision=lax.Precision.HIGHEST,
        preferred_element_type=jnp.float32,
    )


def shards(eigvecs, reflectors, factors):
    blocks = reflectors.shape[0]
    current = eigvecs
    for index in range(blocks - 1, -1, -1):
        panel, factor = (
            lax.all_gather(reflectors[index], "col", axis=0, tiled=True),
            lax.all_gather(factors[index], "col", axis=0, tiled=True),
        )
        partial_value = inner_last(current, panel)
        inner = lax.psum(partial_value, "row")
        scaled = inner_last(inner, factor)
        current = current - matmul(scaled, panel)
    return current


def solution(mesh):
    placed = (P("col", "row"), P(None, "col", "row"), P(None, "col", None))
    return jax.shard_map(
        shards, mesh=mesh, in_specs=placed, out_specs=P("col", "row"), check_vma=False
    )
```

profile of v0, /device:TPU:1, one launch (start us, length us, event | category | flops | bytes accessed | tf_op | source)
XLA Modules:
  0.0 674.6 jit_solution(9740838645187987536)
XLA Ops:
  6.5 0.0 all-gather.10.cloned.1.call-start
  6.5 5.8 fusion.15
  12.3 0.0 all-gather.10.cloned.1.call-update
  12.3 0.0 copy-start
  12.3 0.0 all-reduce.4.cloned.1.call-start
  12.4 153.7 %all-gather.10.cloned.1.call-done = f32[1,256,16384]{2,1,0:T(8,128)} async-done(((f32[1,32,16384]{2,1,0:T(8,128)}), f32[1,256,16384]{2,1,0:T(8,128)}) %all-gather.10.cloned.1.call-update) | async-done | bytes 16777232 | tf_op jit(solution)/shard_map/all_gather | solution.py:26
  166.1 20.2 %fusion.7 = f32[64,256]{1,0:T(8,128)} fusion(f32[64,16384]{1,0:T(8,128)} %param.3, f32[1,256,16384]{2,1,0:T(8,128)} %all-gather.10.cloned.1.call-done), kind=kOutput, calls=%fused_computation.10 | convolution fusion | flops 3221225472 | bytes 21037056 | tf_op jit(solution)/shard_map/dot_general | solution.py:12
  186.3 0.0 all-reduce.4.cloned.1.call-update
  186.3 0.0 all-gather.12.cloned.1.call-start
  186.4 0.7 all-gather.12.cloned.1.call-update
  187.0 0.0 all-reduce.6.cloned.1.call-start
  187.1 0.0 copy-done
  187.1 14.5 %all-gather.1 = f32[1,256,256]{2,1,0:T(8,128)S(1)} all-gather(f32[1,32,256]{2,1,0:T(8,128)S(1)} %get-tuple-element.9), channel_id=3, replica_groups=mesh['row'=4,'col'=8] {'col'}, dimensions={1}, use_global_device_ids=true | all-gather | bytes 294912 | tf_op jit(solution)/shard_map/all_gather | solution.py:27
  201.6 23.7 %all-reduce.4.cloned.1.call-done = f32[64,256]{1,0:T(8,128)} async-done(((f32[64,256]{1,0:T(8,128)}), f32[64,256]{1,0:T(8,128)}) %all-reduce.4.cloned.1.call-update) | async-done | bytes 65552 | tf_op jit(solution)/shard_map/psum | solution.py:30
  225.4 1.2 fusion.13
  226.6 15.6 %convolution_subtract_fusion.2 = f32[64,16384]{1,0:T(8,128)} fusion(f32[64,16384]{1,0:T(8,128)} %param.3, f32[64,256]{1,0:T(8,128)S(1)} %fusion.13, f32[1,256,16384]{2,1,0:T(8,128)} %all-gather.10.cloned.1.call-done), kind=kOutput, calls=%fused_computation.2 | convolution fusion | flops 3222274048 | bytes 25231360 | tf_op jit(solution)/shard_map/dot_general | solution.py:8
  242.2 136.9 %all-gather.12.cloned.1.call-done = f32[1,256,16384]{2,1,0:T(8,128)} async-done(((f32[1,32,16384]{2,1,0:T(8,128)}), f32[1,256,16384]{2,1,0:T(8,128)}) %all-gather.12.cloned.1.call-update) | async-done | bytes 16777232 | tf_op jit(solution)/shard_map/all_gather | solution.py:26
  379.0 20.2 %fusion.4 = f32[64,256]{1,0:T(8,128)} fusion(f32[64,16384]{1,0:T(8,128)} %convolution_subtract_fusion.2, f32[1,256,16384]{2,1,0:T(8,128)} %all-gather.12.cloned.1.call-done), kind=kOutput, calls=%fused_computation.7 | convolution fusion | flops 3221225472 | bytes 21037056 | tf_op jit(solution)/shard_map/dot_general | solution.py:12
  399.2 0.0 all-reduce.6.cloned.1.call-update
  399.2 0.0 all-gather.14.cloned.1.call-start
  399.2 0.5 all-gather.14.cloned.1.call-update
  399.8 0.0 all-reduce.8.cloned.1.call-start
  399.8 14.6 %all-gather.3 = f32[1,256,256]{2,1,0:T(8,128)S(1)} all-gather(f32[1,32,256]{2,1,0:T(8,128)S(1)} %get-tuple-element.10), channel_id=5, replica_groups=mesh['row'=4,'col'=8] {'col'}, dimensions={1}, use_global_device_ids=true | all-gather | bytes 294912 | tf_op jit(solution)/shard_map/all_gather | solution.py:27
  414.4 23.9 %all-reduce.6.cloned.1.call-done = f32[64,256]{1,0:T(8,128)} async-done(((f32[64,256]{1,0:T(8,128)}), f32[64,256]{1,0:T(8,128)}) %all-reduce.6.cloned.1.call-update) | async-done | bytes 65552 | tf_op jit(solution)/shard_map/psum | solution.py:30
  438.3 1.2 fusion.11
  439.5 15.6 %convolution_subtract_fusion.1 = f32[64,16384]{1,0:T(8,128)} fusion(f32[64,16384]{1,0:T(8,128)} %convolution_subtract_fusion.2, f32[64,256]{1,0:T(8,128)S(1)} %fusion.11, f32[1,256,16384]{2,1,0:T(8,128)} %all-gather.12.cloned.1.call-done), kind=kOutput, calls=%fused_computation.1 | convolution fusion | flops 3222274048 | bytes 25231360 | tf_op jit(solution)/shard_map/dot_general | solution.py:8
  455.1 136.6 %all-gather.14.cloned.1.call-done = f32[1,256,16384]{2,1,0:T(8,128)} async-done(((f32[1,32,16384]{2,1,0:T(8,128)}), f32[1,256,16384]{2,1,0:T(8,128)}) %all-gather.14.cloned.1.call-update) | async-done | bytes 16777232 | tf_op jit(solution)/shard_map/all_gather | solution.py:26
  591.7 20.2 %fusion.1 = f32[64,256]{1,0:T(8,128)} fusion(f32[64,16384]{1,0:T(8,128)} %convolution_subtract_fusion.1, f32[1,256,16384]{2,1,0:T(8,128)} %all-gather.14.cloned.1.call-done), kind=kOutput, calls=%fused_computation.4 | convolution fusion | flops 3221225472 | bytes 21037056 | tf_op jit(solution)/shard_map/dot_general | solution.py:12
  611.8 0.0 all-reduce.8.cloned.1.call-update
  611.9 14.6 %all-gather.5 = f32[1,256,256]{2,1,0:T(8,128)S(1)} all-gather(f32[1,32,256]{2,1,0:T(8,128)S(1)} %get-tuple-element.8), channel_id=7, replica_groups=mesh['row'=4,'col'=8] {'col'}, dimensions={1}, use_global_device_ids=true | all-gather | bytes 294912 | tf_op jit(solution)/shard_map/all_gather | solution.py:27
  626.5 24.5 %all-reduce.8.cloned.1.call-done = f32[64,256]{1,0:T(8,128)} async-done(((f32[64,256]{1,0:T(8,128)}), f32[64,256]{1,0:T(8,128)}) %all-reduce.8.cloned.1.call-update) | async-done | bytes 65552 | tf_op jit(solution)/shard_map/psum | solution.py:30
  650.9 1.2 fusion.9
  652.1 15.6 %convolution_subtract_fusion = f32[64,16384]{1,0:T(8,128)} fusion(f32[64,16384]{1,0:T(8,128)} %convolution_subtract_fusion.1, f32[64,256]{1,0:T(8,128)S(1)} %fusion.9, f32[1,256,16384]{2,1,0:T(8,128)} %all-gather.14.cloned.1.call-done), kind=kOutput, calls=%fused_computation | convolution fusion | flops 3222274048 | bytes 25231360 | tf_op jit(solution)/shard_map/dot_general | solution.py:8
  (1 shorter events, 0.0 us)
Async XLA Ops:
  6.5 159.6 %all-gather.10.cloned.1.call-start = ((), (), s32[]{:S(2)}) async-start(), calls=%async_computation.3 | async-start | bytes 18874368 | tf_op jit(solution)/shard_map/all_gather | solution.py:26
  12.3 174.8 %copy-start = (f32[3,32,256]{2,1,0:T(8,128)S(1)}, f32[3,32,256]{2,1,0:T(8,128)}, u32[]{:S(2)}) copy-start(f32[3,32,256]{2,1,0:T(8,128)} %param.5) | copy-start | bytes 294916
  12.3 213.0 %all-reduce.4.cloned.1.call-start = ((), (), s32[]{:S(2)}) async-start(), calls=%async_computation | async-start | bytes 131072 | tf_op jit(solution)/shard_map/psum | solution.py:30
  186.3 192.7 %all-gather.12.cloned.1.call-start = ((), (), s32[]{:S(2)}) async-start(), calls=%async_computation.4 | async-start | bytes 18874368 | tf_op jit(solution)/shard_map/all_gather | solution.py:26
  187.0 251.2 %all-reduce.6.cloned.1.call-start = ((), (), s32[]{:S(2)}) async-start(), calls=%async_computation.1 | async-start | bytes 131072 | tf_op jit(solution)/shard_map/psum | solution.py:30
  399.2 192.5 %all-gather.14.cloned.1.call-start = ((), (), s32[]{:S(2)}) async-start(), calls=%async_computation.5 | async-start | bytes 18874368 | tf_op jit(solution)/shard_map/all_gather | solution.py:26
  399.8 251.1 %all-reduce.8.cloned.1.call-start = ((), (), s32[]{:S(2)}) async-start(), calls=%async_computation.2 | async-start | bytes 131072 | tf_op jit(solution)/shard_map/psum | solution.py:30
Sparse Core Ops, SparseCore 0:
  12.5 153.6 all-gather.9
  186.4 38.8 all-reduce.3
  227.1 151.9 all-gather.11
  399.3 38.9 all-reduce.5
  439.7 151.8 all-gather.13
  612.0 38.8 all-reduce.7
where the time goes:
time: 676 us; the launch traced here: 675 us
  waiting for transfers between devices  501 us (74%)
  matrix products  111 us (16%)
  blocking collectives  43.7 us (6%)
  between operations  13.5 us (2%)
    all_gather x3, waiting for transfers between devices, shards(): lax.all_gather(reflectors[index], 'col', axis=0, tiled=True)  427 us
    psum x3, waiting for transfers between devices, shards(): inner = lax.psum(partial_value, 'row')  72.1 us
    dot_general x6, matrix products, inner_last(): lax.dot_general(left, right, (((1,), (1,)), ((), ())), precision=lax.Prec...  64.1 us
    dot_general x3, matrix products, matmul(): jnp.dot(left, right, precision=lax.Precision.HIGHEST, preferred_element_t...  46.8 us
    all_gather x3, blocking collectives, shards(): lax.all_gather(factors[index], 'col', axis=0, tiled=True)  43.7 us
  transfers between devices with their start and end apart: 6, of which 6 were waited for; matrix products, arithmetic and copies ran while one was open for 5% of the time, Pallas kernels for 0%

commit v1 on v0

v1 whole, which is shorter than its diff:
```python
import functools

import jax
import jax.numpy as jnp
from jax import lax
from jax.experimental import pallas as pl
from jax.experimental.pallas import tpu as pltpu
from jax.sharding import PartitionSpec as P

MESH = pl.DeviceIdType.MESH
HIGHEST = lax.Precision.HIGHEST


def product(left, right):
    return lax.dot_general(
        left, right, (((1,), (0,)), ((), ())), precision=HIGHEST, preferred_element_type=jnp.float32
    )


def product_last(left, right):
    return lax.dot_general(
        left, right, (((1,), (1,)), ((), ())), precision=HIGHEST, preferred_element_type=jnp.float32
    )


def await_bytes(ref, sem):
    pltpu.make_async_copy(ref, ref, sem).wait()


def kernel(
    rows, cols, group, tile,
    eig_ref, refl_ref, fact_ref, out_ref,
    panel, cur, fact, inner, part, parts, mine, pieces, scaled,
    fact_send, fact_recv, cur_send, cur_recv, panel_send, panel_recv,
    part_send, part_recv, scal_send, scal_recv, out_send, out_recv,
):
    blocks, depth, extent = refl_ref.shape
    vectors = eig_ref.shape[0]
    width = extent // group
    members = rows * group
    height = vectors * group // members
    row, col = lax.axis_index("row"), lax.axis_index("col")
    team, seat = col // group, col % group
    rank = row * group + seat

    def remote(src, dst, send, recv, to):
        pltpu.make_async_remote_copy(
            src_ref=src, dst_ref=dst, send_sem=send, recv_sem=recv, device_id=to, device_id_type=MESH
        ).start()

    def member(step):
        other = (rank + step) % members
        return other, (other // group, team * group + other % group)

    def cut(index):
        return pl.ds(pl.multiple_of(index * width, width), width)

    def own(index, size):
        return pl.ds(pl.multiple_of(index * size, size), size)

    def outside(step):
        return ((team + 1) * group + (step + seat) % (cols - group)) % cols

    def inside(step):
        return team * group + (seat + step) % group

    barrier = pltpu.get_barrier_semaphore()

    @pl.loop(1, members)
    def _(step):
        pl.semaphore_signal(barrier, inc=1, device_id=member(step)[1], device_id_type=MESH)

    @pl.loop(0, cols - group)
    def _(step):
        pl.semaphore_signal(barrier, inc=1, device_id=(row, outside(step)), device_id_type=MESH)

    pl.semaphore_wait(barrier, members - 1 + cols - group)

    def send_panel(index, other):
        remote(
            refl_ref.at[index, :, cut(other % group)], panel.at[index, own(col, depth), :],
            panel_send.at[index], panel_recv.at[index], (row, other),
        )

    def send_fact(other):
        remote(fact_ref, fact.at[:, own(col, depth), :], fact_send, fact_recv, (row, other))

    @pl.loop(1, group)
    def _(step):
        other = inside(step)
        remote(
            eig_ref.at[:, cut(other % group)], cur.at[own(seat, vectors), :], cur_send, cur_recv, (row, other)
        )

    for index in range(blocks - 1, -1, -1):
        @pl.loop(0, cols - group)
        def _(step):
            send_panel(index, outside(step))

        @pl.loop(1, group)
        def _(step):
            send_panel(index, inside(step))

        pltpu.make_async_copy(
            refl_ref.at[index, :, cut(seat)], panel.at[index, own(col, depth), :], panel_recv.at[index]
        ).start()
        if index == blocks - 1:
            @pl.loop(0, cols - group)
            def _(step):
                send_fact(outside(step))

            @pl.loop(1, group)
            def _(step):
                send_fact(inside(step))

            pltpu.make_async_copy(fact_ref, fact.at[:, own(col, depth), :], fact_recv).start()
            pltpu.make_async_copy(eig_ref.at[:, cut(seat)], cur.at[own(seat, vectors), :], cur_recv).start()

    await_bytes(cur, cur_recv)
    for index in range(blocks - 1, -1, -1):
        await_bytes(panel.at[index], panel_recv.at[index])
        inner[...] = jnp.zeros_like(inner)

        @pl.loop(0, width // tile)
        def _(step):
            at = pl.ds(pl.multiple_of(step * tile, tile), tile)
            inner[...] += product_last(cur[:, at], panel[index, :, at])

        for other in range(members):
            part[index, other] = inner[pl.ds(other * height, height), :]

        @pl.loop(1, members)
        def _(step):
            other, to = member(step)
            remote(part.at[index, other], parts.at[index, rank], part_send.at[index], part_recv.at[index], to)

        pltpu.make_async_copy(part.at[index, rank], parts.at[index, rank], part_recv.at[index]).start()
        if index == blocks - 1:
            await_bytes(fact, fact_recv)
        await_bytes(parts.at[index], part_recv.at[index])
        total = parts[index, 0]
        for other in range(1, members):
            total = total + parts[index, other]
        mine[index] = product_last(total, fact[index])

        @pl.loop(1, members)
        def _(step):
            remote(
                mine.at[index], pieces.at[index, rank], scal_send.at[index], scal_recv.at[index], member(step)[1]
            )

        pltpu.make_async_copy(mine.at[index], pieces.at[index, rank], scal_recv.at[index]).start()
        await_bytes(pieces.at[index], scal_recv.at[index])
        for other in range(members):
            scaled[pl.ds(other * height, height), :] = pieces[index, other]

        @pl.loop(0, width // tile)
        def _(step):
            at = pl.ds(pl.multiple_of(step * tile, tile), tile)
            cur[:, at] = cur[:, at] - product(scaled[...], panel[index, :, at])
            if index == 0:
                to_at = pl.ds(pl.multiple_of(seat * width + step * tile, tile), tile)

                @pl.loop(1, group)
                def _(hop):
                    other = inside(hop)
                    remote(
                        cur.at[own(other % group, vectors), at], out_ref.at[:, to_at], out_send, out_recv,
                        (row, other),
                    )

                pltpu.make_async_copy(cur.at[own(seat, vectors), at], out_ref.at[:, to_at], out_recv).start()

    await_bytes(out_ref, out_recv)
    await_bytes(cur.at[pl.ds(0, (group - 1) * vectors), :], out_send)
    await_bytes(cur.at[pl.ds(0, (group - 1) * vectors), :], cur_send)
    await_bytes(fact.at[:, pl.ds(0, (cols - 1) * depth), :], fact_send)
    for index in range(blocks):
        await_bytes(panel.at[index, pl.ds(0, (cols - 1) * depth), :], panel_send.at[index])
        await_bytes(parts.at[index, pl.ds(0, members - 1)], part_send.at[index])
        await_bytes(pieces.at[index, pl.ds(0, members - 1)], scal_send.at[index])


def shards(rows, cols, eigvecs, reflectors, factors):
    vectors, extent = eigvecs.shape
    blocks, depth, _ = reflectors.shape
    order = depth * cols
    group = min(4, cols // 2)
    width = extent // group
    tile = min(512, width)
    members = rows * group
    height = vectors * group // members
    dma = pltpu.SemaphoreType.DMA
    anywhere = pl.BlockSpec(memory_space=pl.ANY)
    exchanged = (blocks, members, height, order)
    return pl.pallas_call(
        functools.partial(kernel, rows, cols, group, tile),
        out_shape=jax.ShapeDtypeStruct(eigvecs.shape, jnp.float32),
        in_specs=[anywhere] * 3,
        out_specs=anywhere,
        scratch_shapes=[
            pltpu.VMEM((blocks, order, width), jnp.float32),
            pltpu.VMEM((vectors * group, width), jnp.float32),
            pltpu.VMEM((blocks, order, order), jnp.float32),
            pltpu.VMEM((vectors * group, order), jnp.float32),
            pltpu.VMEM(exchanged, jnp.float32),
            pltpu.VMEM(exchanged, jnp.float32),
            pltpu.VMEM((blocks, height, order), jnp.float32),
            pltpu.VMEM(exchanged, jnp.float32),
            pltpu.VMEM((vectors * group, order), jnp.float32),
            dma, dma, dma, dma, dma((blocks,)), dma((blocks,)),
            dma((blocks,)), dma((blocks,)), dma((blocks,)), dma((blocks,)), dma, dma,
        ],
        compiler_params=pltpu.CompilerParams(
            collective_id=0, has_side_effects=True, vmem_limit_bytes=52 * 1024 * 1024
        ),
        cost_estimate=pl.CostEstimate(
            flops=4 * blocks * vectors * group * order * width, bytes_accessed=4 * 6 * blocks * order * width,
            transcendentals=0,
        ),
    )(eigvecs, reflectors, factors)


def solution(mesh):
    placed = (P("col", "row"), P(None, "col", "row"), P(None, "col", None))
    return jax.shard_map(
        functools.partial(shards, mesh.shape["row"], mesh.shape["col"]),
        mesh=mesh, in_specs=placed, out_specs=P("col", "row"), check_vma=False,
    )
```

time: 676 us -> 373 us (0.55)
  waiting for transfers between devices: 501 us -> 0 us
  Pallas kernels: 0 us -> 367 us
  matrix products: 111 us -> 0 us
  blocking collectives: 43.7 us -> 0 us
  between operations: 13.5 us -> 0.01 us
    all_gather x3 -> x0, waiting for transfers between devices: 427 us -> none  [shards(): lax.all_gather(reflectors[index], 'col', axis=0, tiled=True)]
    pallas_call x0 -> x1, Pallas kernels: none -> 367 us  [shards(): pl.pallas_call(functools.partial(kernel, rows, cols, group, tile), out_sh...]
    dot_general x9 -> x0, matrix products: 111 us -> none  [the longest x6 64.1 us: inner_last(): lax.dot_general(left, right, (((1,), (1,)), ((), ())), precision=lax.Prec...]
    psum x3 -> x0, waiting for transfers between devices: 72.1 us -> none  [shards(): inner = lax.psum(partial_value, 'row')]
    all_gather x3 -> x0, blocking collectives: 43.7 us -> none  [shards(): lax.all_gather(factors[index], 'col', axis=0, tiled=True)]
  transfers between devices with their start and end apart: 6 -> 0, of which waited for: 6 -> 0; matrix products, arithmetic and copies ran while one was open for 5% -> 0% of each run, Pallas kernels for 0% -> 0%
where the time goes in v1:
time: 373 us; the launch traced here: 372 us
  Pallas kernels  367 us (98%)
  local copies, waits for them, and re-layouts  5.4 us (1%)
    pallas_call x1, Pallas kernels, shards(): pl.pallas_call(functools.partial(kernel, rows, cols, group, tile), out_sh...  367 us

profile of v1, /device:TPU:1, one launch (start us, length us, event | category | flops | bytes accessed | tf_op | source)
XLA Modules:
  0.0 372.4 jit_solution(325656530100213742)
XLA Ops:
  0.0 0.0 copy-start
  0.0 0.9 copy-done
  0.9 367.0 %shard_map.37 = f32[64,16384]{1,0:T(8,128)} custom-call(f32[64,16384]{1,0:T(8,128)} %eig_ref.1, f32[3,32,16384]{2,1,0:T(8,128)} %refl_ref.1, f32[3,32,256]{2,1,0:T(8,128)S(1)} %copy-done), custom_call_target="tpu_custom_call" | custom-call | flops 3221225472 | bytes 75497472 | tf_op jit(solution)/shard_map/pallas_call | solution.py:196
  367.9 4.5 %copy.5 = f32[64,16384]{1,0:T(8,128)} copy(f32[64,16384]{1,0:T(8,128)} %shard_map.37) | data formatting | bytes 8388608
Async XLA Ops:
  0.0 0.9 copy-start

commit v2 on v1

--- a/solution.py
+++ b/solution.py
@@ -11,27 +11,41 @@
 HIGHEST = lax.Precision.HIGHEST
 
 
+def split(value):
+    high = value.astype(jnp.bfloat16)
+    return high, (value - high.astype(jnp.float32)).astype(jnp.bfloat16)
+
+
+def contract(left, right, dim):
+    (left_high, left_low), (right_high, right_low) = split(left), split(right)
+
+    def dot(one, other):
+        return lax.dot_general(one, other, (((1,), (dim,)), ((), ())), preferred_element_type=jnp.float32)
+
+    return dot(left_high, right_high) + (dot(left_high, right_low) + dot(left_low, right_high))
+
+
 def product(left, right):
-    return lax.dot_general(
-        left, right, (((1,), (0,)), ((), ())), precision=HIGHEST, preferred_element_type=jnp.float32
-    )
+    return contract(left, right, 0)
 
 
 def product_last(left, right):
-    return lax.dot_general(
-        left, right, (((1,), (1,)), ((), ())), precision=HIGHEST, preferred_element_type=jnp.float32
-    )
+    return contract(left, right, 1)
 
 
 def await_bytes(ref, sem):
     pltpu.make_async_copy(ref, ref, sem).wait()
 
 
+def factor_ways(rows, depth):
+    return rows if depth % (8 * rows) == 0 else 1
+
+
 def kernel(
-    rows, cols, group, tile,
+    rows, cols, group, tile, slices,
     eig_ref, refl_ref, fact_ref, out_ref,
-    panel, cur, fact, inner, part, parts, mine, pieces, scaled,
-    fact_send, fact_recv, cur_send, cur_recv, panel_send, panel_recv,
+    panel, cur, fact, shares, inner, part, parts, mine, pieces, scaled,
+    fact_send, fact_recv, share_send, share_recv, cur_send, cur_recv, panel_send, panel_recv,
     part_send, part_recv, scal_send, scal_recv, out_send, out_recv,
 ):
     blocks, depth, extent = refl_ref.shape
@@ -42,6 +56,10 @@
     row, col = lax.axis_index("row"), lax.axis_index("col")
     team, seat = col // group, col % group
     rank = row * group + seat
+    ways = factor_ways(rows, depth)
+    share = depth // ways
+    way = row % ways
+    slice_width = width // slices
 
     def remote(src, dst, send, recv, to):
         pltpu.make_async_remote_copy(
@@ -76,55 +94,86 @@
 
     pl.semaphore_wait(barrier, members - 1 + cols - group)
 
-    def send_panel(index, other):
+    def parts_of(index):
+        count = slices if index == 0 else 1
+        return [(at, width // count) for at in range(count)]
+
+    def panel_at(index, at, size):
+        return panel.at[index, own(col, depth), pl.ds(at * size, size)]
+
+    def panel_from(index, at, size, other):
+        start = pl.multiple_of(other % group * width + at * size, size)
+        return refl_ref.at[index, :, pl.ds(start, size)]
+
+    def send_panel(index, at, size, other):
         remote(
-            refl_ref.at[index, :, cut(other % group)], panel.at[index, own(col, depth), :],
-            panel_send.at[index], panel_recv.at[index], (row, other),
+            panel_from(index, at, size, other), panel_at(index, at, size),
+            panel_send.at[index], panel_recv.at[index, at], (row, other),
         )
 
-    def send_fact(other):
-        remote(fact_ref, fact.at[:, own(col, depth), :], fact_send, fact_recv, (row, other))
+    def my_share():
+        return fact_ref.at[:, own(way, share), :]
+
+    def send_share(other):
+        remote(my_share(), shares.at[way, :, col], fact_send, fact_recv, (row, other))
+
+    @pl.loop(0, cols - group)
+    def _(step):
+        send_share(outside(step))
 
     @pl.loop(1, group)
     def _(step):
-        other = inside(step)
-        remote(
-            eig_ref.at[:, cut(other % group)], cur.at[own(seat, vectors), :], cur_send, cur_recv, (row, other)
-        )
+        send_share(inside(step))
+
+    pltpu.make_async_copy(my_share(), shares.at[way, :, col], fact_recv).start()
+    pltpu.make_async_copy(eig_ref.at[:, cut(seat)], cur.at[own(seat, vectors), :], cur_recv).start()
 
     for index in range(blocks - 1, -1, -1):
-        @pl.loop(0, cols - group)
-        def _(step):
-            send_panel(index, outside(step))
-
-        @pl.loop(1, group)
-        def _(step):
-            send_panel(index, inside(step))
-
-        pltpu.make_async_copy(
-            refl_ref.at[index, :, cut(seat)], panel.at[index, own(col, depth), :], panel_recv.at[index]
-        ).start()
-        if index == blocks - 1:
+        for at, size in parts_of(index):
             @pl.loop(0, cols - group)
             def _(step):
-                send_fact(outside(step))
+                send_panel(index, at, size, outside(step))
+
+            if index == blocks - 1:
+                @pl.loop(1, group)
+                def _(step):
+                    other = inside(step)
+                    remote(
+                        eig_ref.at[:, cut(other % group)], cur.at[own(seat, vectors), :], cur_send, cur_recv,
+                        (row, other),
+                    )
 
             @pl.loop(1, group)
             def _(step):
-                send_fact(inside(step))
-
-            pltpu.make_async_copy(fact_ref, fact.at[:, own(col, depth), :], fact_recv).start()
-            pltpu.make_async_copy(eig_ref.at[:, cut(seat)], cur.at[own(seat, vectors), :], cur_recv).start()
+                send_panel(index, at, size, inside(step))
+
+            pltpu.make_async_copy(
+                panel_from(index, at, size, col), panel_at(index, at, size), panel_recv.at[index, at]
+            ).start()
+
+    await_bytes(shares.at[way], fact_recv)
+    if ways > 1:
+        @pl.loop(1, ways)
+        def _(step):
+            remote(shares.at[way], shares.at[way], share_send, share_recv, ((row + step) % ways, col))
+
+        await_bytes(shares.at[pl.ds(0, ways - 1)], share_recv)
+
+    for index in range(blocks):
+        for owner in range(cols):
+            for at in range(ways):
+                fact[index, pl.ds(owner * depth + at * share, share), :] = shares[at, index, owner]
 
     await_bytes(cur, cur_recv)
     for index in range(blocks - 1, -1, -1):
-        await_bytes(panel.at[index], panel_recv.at[index])
         inner[...] = jnp.zeros_like(inner)
-
-        @pl.loop(0, width // tile)
-        def _(step):
-            at = pl.ds(pl.multiple_of(step * tile, tile), tile)
-            inner[...] += product_last(cur[:, at], panel[index, :, at])
+        for number, size in parts_of(index):
+            await_bytes(panel.at[index, :, pl.ds(number * size, size)], panel_recv.at[index, number])
+
+            @pl.loop(0, size // tile)
+            def _(step):
+                at = pl.ds(pl.multiple_of(number * size + step * tile, tile), tile)
+                inner[...] += product_last(cur[:, at], panel[index, :, at])
 
         for other in range(members):
             part[index, other] = inner[pl.ds(other * height, height), :]
@@ -135,8 +184,6 @@
             remote(part.at[index, other], parts.at[index, rank], part_send.at[index], part_recv.at[index], to)
 
         pltpu.make_async_copy(part.at[index, rank], parts.at[index, rank], part_recv.at[index]).start()
-        if index == blocks - 1:
-            await_bytes(fact, fact_recv)
         await_bytes(parts.at[index], part_recv.at[index])
         total = parts[index, 0]
         for other in range(1, members):
@@ -174,7 +221,9 @@
     await_bytes(out_ref, out_recv)
     await_bytes(cur.at[pl.ds(0, (group - 1) * vectors), :], out_send)
     await_bytes(cur.at[pl.ds(0, (group - 1) * vectors), :], cur_send)
-    await_bytes(fact.at[:, pl.ds(0, (cols - 1) * depth), :], fact_send)
+    await_bytes(shares.at[way, :, pl.ds(0, cols - 1)], fact_send)
+    if ways > 1:
+        await_bytes(shares.at[pl.ds(0, ways - 1)], share_send)
     for index in range(blocks):
         await_bytes(panel.at[index, pl.ds(0, (cols - 1) * depth), :], panel_send.at[index])
         await_bytes(parts.at[index, pl.ds(0, members - 1)], part_send.at[index])
@@ -192,9 +241,11 @@
     height = vectors * group // members
     dma = pltpu.SemaphoreType.DMA
     anywhere = pl.BlockSpec(memory_space=pl.ANY)
+    ways = factor_ways(rows, depth)
+    slices = max(1, min(4, width // tile))
     exchanged = (blocks, members, height, order)
     return pl.pallas_call(
-        functools.partial(kernel, rows, cols, group, tile),
+        functools.partial(kernel, rows, cols, group, tile, slices),
         out_shape=jax.ShapeDtypeStruct(eigvecs.shape, jnp.float32),
         in_specs=[anywhere] * 3,
         out_specs=anywhere,
@@ -202,13 +253,14 @@
             pltpu.VMEM((blocks, order, width), jnp.float32),
             pltpu.VMEM((vectors * group, width), jnp.float32),
             pltpu.VMEM((blocks, order, order), jnp.float32),
+            pltpu.VMEM((ways, blocks, cols, depth // ways, order), jnp.float32),
             pltpu.VMEM((vectors * group, order), jnp.float32),
             pltpu.VMEM(exchanged, jnp.float32),
             pltpu.VMEM(exchanged, jnp.float32),
             pltpu.VMEM((blocks, height, order), jnp.float32),
             pltpu.VMEM(exchanged, jnp.float32),
             pltpu.VMEM((vectors * group, order), jnp.float32),
-            dma, dma, dma, dma, dma((blocks,)), dma((blocks,)),
+            dma, dma, dma, dma, dma, dma, dma((blocks,)), dma((blocks, slices)),
             dma((blocks,)), dma((blocks,)), dma((blocks,)), dma((blocks,)), dma, dma,
         ],
         compiler_params=pltpu.CompilerParams(

time: 373 us -> 354 us (0.949)
  Pallas kernels: 367 us -> 349 us
    pallas_call x1, Pallas kernels: 367 us -> 349 us  [shards(): pl.pallas_call(functools.partial(kernel, rows, cols, group, tile, slices)...]
where the time goes in v2:
time: 354 us
  Pallas kernels  349 us (99%)
  local copies, waits for them, and re-layouts  5.4 us (2%)
    pallas_call x1, Pallas kernels, shards(): pl.pallas_call(functools.partial(kernel, rows, cols, group, tile, slices)...  349 us

profile of v2, /device:TPU:1, one launch (start us, length us, event | category | flops | bytes accessed | tf_op | source)
XLA Modules:
  0.0 354.2 jit_solution(17151162808473705403)
XLA Ops:
  0.0 0.0 copy-start
  0.0 0.9 copy-done
  0.9 348.7 %shard_map.37 = f32[64,16384]{1,0:T(8,128)} custom-call(f32[64,16384]{1,0:T(8,128)} %eig_ref.1, f32[3,32,16384]{2,1,0:T(8,128)} %refl_ref.1, f32[3,32,256]{2,1,0:T(8,128)S(1)} %copy-done), custom_call_target="tpu_custom_call" | custom-call | flops 3221225472 | bytes 75497472 | tf_op jit(solution)/shard_map/pallas_call | solution.py:247
  349.6 4.5 %copy.5 = f32[64,16384]{1,0:T(8,128)} copy(f32[64,16384]{1,0:T(8,128)} %shard_map.37) | data formatting | bytes 8388608
Async XLA Ops:
  0.0 0.9 copy-start

commit v3 on v2

--- a/solution.py
+++ b/solution.py
@@ -117,14 +117,6 @@
     def send_share(other):
         remote(my_share(), shares.at[way, :, col], fact_send, fact_recv, (row, other))
 
-    @pl.loop(0, cols - group)
-    def _(step):
-        send_share(outside(step))
-
-    @pl.loop(1, group)
-    def _(step):
-        send_share(inside(step))
-
     pltpu.make_async_copy(my_share(), shares.at[way, :, col], fact_recv).start()
     pltpu.make_async_copy(eig_ref.at[:, cut(seat)], cur.at[own(seat, vectors), :], cur_recv).start()
 
@@ -135,6 +127,14 @@
                 send_panel(index, at, size, outside(step))
 
             if index == blocks - 1:
+                @pl.loop(0, cols - group)
+                def _(step):
+                    send_share(outside(step))
+
+                @pl.loop(1, group)
+                def _(step):
+                    send_share(inside(step))
+
                 @pl.loop(1, group)
                 def _(step):
                     other = inside(step)
@@ -236,7 +236,7 @@
     order = depth * cols
     group = min(4, cols // 2)
     width = extent // group
-    tile = min(512, width)
+    tile = min(1024, width)
     members = rows * group
     height = vectors * group // members
     dma = pltpu.SemaphoreType.DMA

time: 354 us -> 354 us (level)
  no operation moved by 1% of the time
where the time goes in v3:
time: 354 us
  Pallas kernels  348 us (98%)
  local copies, waits for them, and re-layouts  5.4 us (2%)
    pallas_call x1, Pallas kernels, shards(): pl.pallas_call(functools.partial(kernel, rows, cols, group, tile, slices)...  348 us

profile of v3, /device:TPU:1, one launch (start us, length us, event | category | flops | bytes accessed | tf_op | source)
XLA Modules:
  0.0 353.5 jit_solution(8082802262964132043)
XLA Ops:
  0.0 0.0 copy-start
  0.0 0.9 copy-done
  0.9 348.1 %shard_map.37 = f32[64,16384]{1,0:T(8,128)} custom-call(f32[64,16384]{1,0:T(8,128)} %eig_ref.1, f32[3,32,16384]{2,1,0:T(8,128)} %refl_ref.1, f32[3,32,256]{2,1,0:T(8,128)S(1)} %copy-done), custom_call_target="tpu_custom_call" | custom-call | flops 3221225472 | bytes 75497472 | tf_op jit(solution)/shard_map/pallas_call | solution.py:247
  349.0 4.5 %copy.5 = f32[64,16384]{1,0:T(8,128)} copy(f32[64,16384]{1,0:T(8,128)} %shard_map.37) | data formatting | bytes 8388608
Async XLA Ops:
  0.0 0.9 copy-start
